TPU v7x, 32 devices: a whole 2x2x4 slice. The times are simulated.
32 devices in a mesh: groups: 2 (over x), dp: 2 (over core), loop: 8 (over z, y).
Axes of the slice: x: 2, y: 2, z: 4, core: 2. Of those that a mesh axis runs over, the one named last changes fastest.
Arguments:
- tokens: bfloat16 [512, 2304], P(('groups', 'dp', 'loop')), parts along dimension 0, may hold values from -6 to 6
- grad_out: bfloat16 [512, 2304], P(('groups', 'dp', 'loop')), parts along dimension 0, may hold values from -6 to 6
- gate_weight: bfloat16 [2304, 18432], P('dp', 'loop'), may hold values from -0.125 to 0.125
- up_weight: bfloat16 [2304, 18432], P('dp', 'loop'), may hold values from -0.125 to 0.125
- down_weight: bfloat16 [18432, 2304], P('loop', 'dp'), may hold values from -0.046875 to 0.046875
Outputs:
- grad_tokens: bfloat16 [512, 2304], P(('groups', 'dp', 'loop')), parts along dimension 0
- grad_gate: float32 [4608, 18432], P(('groups', 'dp'), 'loop'), parts along dimension 0
- grad_up: float32 [4608, 18432], P(('groups', 'dp'), 'loop'), parts along dimension 0
- grad_down: float32 [36864, 2304], P(('groups', 'loop'), 'dp'), parts along dimension 0
There are 2 independent parts, one for each index of `groups`. A program takes and returns all parts, laid end to end along the dimension named above; an argument that names none is the same for every part. Nothing has to cross between parts.
All inputs are finite; a program needn't handle non-finite values.
Results may differ from a plain program's by a relative error of at most 0.005.
Values may be sent and summed in bfloat16 or wider, within the bound.
A program may use at most 256 MiB of HBM per device.

v0:
```python
import jax
import jax.numpy as jnp
from jax import lax
from jax.sharding import PartitionSpec as P


def contract_last(left, right):
    return lax.dot_general(
        left, right, (((1,), (1,)), ((), ())), preferred_element_type=jnp.float32
    )


def contract_first(left, right):
    return lax.dot_general(
        left, right, (((0,), (0,)), ((), ())), preferred_element_type=jnp.float32
    )


def pointwise(gate, up, grad_hidden):
    sigma = jax.nn.sigmoid(gate)
    hidden = (gate * sigma * up).astype(jnp.bfloat16)
    grad_gate_pre = (grad_hidden * up * (sigma + gate * sigma * (1.0 - sigma))).astype(jnp.bfloat16)
    grad_up_pre = (grad_hidden * gate * sigma).astype(jnp.bfloat16)
    return (hidden, grad_gate_pre, grad_up_pre)


def on_device(tokens, grad_out, gate_weight, up_weight, down_weight):
    def halves(rows):
        rows = lax.all_to_all(rows, "dp", split_axis=1, concat_axis=0, tiled=True)
        return lax.all_gather(rows, "loop", axis=0, tiled=True)

    def both(term):
        sent = term.astype(jnp.bfloat16)
        return term + lax.ppermute(sent, "dp", [(0, 1), (1, 0)]).astype(jnp.float32)

    features, upstream = halves(tokens), halves(grad_out)
    gate = both(jnp.dot(features, gate_weight, preferred_element_type=jnp.float32))
    up = both(jnp.dot(features, up_weight, preferred_element_type=jnp.float32))
    grad_hidden = both(contract_last(upstream, down_weight))
    hidden, grad_gate_pre, grad_up_pre = pointwise(gate, up, grad_hidden)
    grad_rows = lax.psum_scatter(
        contract_last(grad_gate_pre, gate_weight) + contract_last(grad_up_pre, up_weight),
        "loop",
        scatter_dimension=0,
        tiled=True,
    ).astype(jnp.bfloat16)
    grad_tokens = lax.all_to_all(grad_rows, "dp", split_axis=0, concat_axis=1, tiled=True)
    grad_gate = contract_first(features, grad_gate_pre)
    grad_up = contract_first(features, grad_up_pre)
    grad_down = contract_first(hidden, upstream)
    return (grad_tokens, grad_gate, grad_up, grad_down)


def solution(mesh):
    in_specs = (
        P(("groups", "dp", "loop"), None),
        P(("groups", "dp", "loop"), None),
        P("dp", "loop"),
        P("dp", "loop"),
        P("loop", "dp"),
    )
    out_specs = (
        P(("groups", "dp", "loop"), None),
        P(("groups", "dp"), "loop"),
        P(("groups", "dp"), "loop"),
        P(("groups", "loop"), "dp"),
    )
    return jax.shard_map(
        on_device, mesh=mesh, in_specs=in_specs, out_specs=out_specs, check_vma=False
    )
```

profile of v0, /device:TPU:0, one launch (start us, length us, event | category | flops | bytes accessed | tf_op | source)
XLA Modules:
  0.0 175.9 jit_solution(3474178678907853698)
XLA Ops:
  7.2 0.0 reduce-scatter.2.cloned.1.call-start
  7.2 0.9 copy.30
  8.1 3.7 %all_to_all.57 = bf16[16,2,1152]{2,0,1:T(8,128)(2,1)S(1)} all-to-all(bf16[16,2,1152]{2,0,1:T(8,128)(2,1)S(1)} %bitcast.41), channel_id=1, replica_groups=mesh['groups'=2,'dp'=2,'loop'=8] {'dp'}, dimensions={1} | all-to-all | bytes 147456 | tf_op jit(solution)/shard_map/all_to_all | solution.py:29
  11.9 33.5 %all_gather.7 = bf16[256,1152]{1,0:T(8,128)(2,1)S(1)} all-gather(bf16[32,1152]{1,0:T(8,128)(2,1)S(1)} %bitcast.43), channel_id=1, replica_groups=mesh['groups'=2,'dp'=2,'loop'=8] {'loop'}, dimensions={0}, use_global_device_ids=true | all-gather | bytes 663552 | tf_op jit(solution)/shard_map/all_gather | solution.py:30
  45.3 4.5 %fusion.6 = (bf16[256,2304]{1,0:T(8,128)(2,1)S(1)}, f32[256,2304]{1,0:T(8,128)S(1)}) fusion(bf16[256,1152]{1,0:T(8,128)(2,1)S(1)} %all_gather.7, bf16[1152,2304]{1,0:T(8,128)(2,1)} %param.8), kind=kOutput, calls=%fused_computation.17 | convolution fusion | flops 1359544320 | bytes 9437184 | tf_op jit(solution)/shard_map/dot_general | solution.py:38
  49.8 0.0 slice-start
  49.9 0.0 copy-start.6
  49.9 0.0 slice-start.1
  49.9 0.1 collective-permute-start.1
  50.0 1.7 fusion.5
  51.7 0.5 collective-permute-start.2
  52.3 3.8 %all_to_all.58 = bf16[16,2,1152]{2,0,1:T(8,128)(2,1)S(1)} all-to-all(bf16[16,2,1152]{2,0,1:T(8,128)(2,1)S(1)} %bitcast.42), channel_id=1, replica_groups=mesh['groups'=2,'dp'=2,'loop'=8] {'dp'}, dimensions={1} | all-to-all | bytes 147456 | tf_op jit(solution)/shard_map/all_to_all | solution.py:29
  56.0 31.7 %all_gather.6 = bf16[256,1152]{1,0:T(8,128)(2,1)S(1)} all-gather(bf16[32,1152]{1,0:T(8,128)(2,1)S(1)} %bitcast.44), channel_id=1, replica_groups=mesh['groups'=2,'dp'=2,'loop'=8] {'loop'}, dimensions={0}, use_global_device_ids=true | all-gather | bytes 663552 | tf_op jit(solution)/shard_map/all_gather | solution.py:30
  87.8 0.0 slice-start.4
  87.8 1.7 fusion.4
  89.5 0.1 collective-permute-start
  89.6 0.0 collective-permute-done.1
  89.6 2.8 %collective-permute-done = bf16[256,2304]{1,0:T(8,128)(2,1)S(1)} collective-permute-done((bf16[256,2304]{1,0:T(8,128)(2,1)S(1)}, bf16[256,2304]{1,0:T(8,128)(2,1)S(1)}, u32[]{:S(2)}, u32[]{:S(2)}) %collective-permute-start) | collective-permute-done | bytes 1179680 | tf_op jit(solution)/shard_map/ppermute | solution.py:34
  92.4 1.5 multiply_convert_fusion.1
  94.0 0.0 copy-start.3
  94.0 1.7 fusion.7
  95.8 2.8 %convolution_add_fusion = f32[256,1152]{1,0:T(8,128)} fusion(f32[256,1152]{1,0:T(8,128)S(1)} %fusion.7, bf16[256,2304]{1,0:T(8,128)(2,1)S(1)} %get-tuple-element.20, bf16[1152,2304]{1,0:T(8,128)(2,1)S(1)} %bitcast.51), kind=kOutput, calls=%fused_computation.2 | convolution fusion | flops 1359249408 | bytes 8847360 | tf_op jit(solution)/shard_map/dot_general | solution.py:8
  98.5 0.0 reduce-scatter.2.cloned.1.call-update
  98.5 7.3 %convolution_bitcast_fusion.1 = f32[1152,2304]{0,1:T(8,128)} fusion(bf16[256,2304]{1,0:T(8,128)(2,1)} %copy-done.3, bf16[256,1152]{1,0:T(8,128)(2,1)} %copy-done.4), kind=kOutput, calls=%fused_computation.1 | convolution fusion | flops 1358954496 | bytes 12386304 | tf_op jit(solution)/shard_map/dot_general | solution.py:14
  105.8 12.8 %copy.23 = f32[1152,2304]{1,0:T(8,128)} copy(f32[1152,2304]{0,1:T(8,128)} %convolution_bitcast_fusion.1) | data formatting | bytes 21233664
  118.6 7.3 %convolution_bitcast_fusion = f32[1152,2304]{0,1:T(8,128)} fusion(bf16[256,2304]{1,0:T(8,128)(2,1)} %copy-done.2, bf16[256,1152]{1,0:T(8,128)(2,1)} %copy-done.4), kind=kOutput, calls=%fused_computation | convolution fusion | flops 1358954496 | bytes 12386304 | tf_op jit(solution)/shard_map/dot_general | solution.py:14
  125.9 12.7 %copy.24 = f32[1152,2304]{1,0:T(8,128)} copy(f32[1152,2304]{0,1:T(8,128)} %convolution_bitcast_fusion) | data formatting | bytes 21233664
  138.6 8.5 %fusion = f32[2304,1152]{1,0:T(8,128)} fusion(bf16[256,1152]{1,0:T(8,128)(2,1)} %copy-done.5, f32[256,2304]{1,0:T(8,128)S(1)} %get-tuple-element.27, bf16[256,2304]{1,0:T(8,128)(2,1)S(1)} %collective-permute-done.1, f32[256,2304]{1,0:T(8,128)} %copy-done, bf16[256,2304]{1,0:T(8,128)(2,1)} %copy-done.1), kind=kOutput, calls=%fused_computation.10 | convolution fusion | flops 1364852736 | bytes 18284544 | tf_op jit(solution)/shard_map/dot_general | solution.py:14
  147.1 16.7 %reduce-scatter.2.cloned.1.call-done = f32[32,1152]{1,0:T(8,128)} async-done(((f32[256,1152]{1,0:T(8,128)}), f32[32,1152]{1,0:T(8,128)}) %reduce-scatter.2.cloned.1.call-update) | async-done | bytes 147472 | tf_op jit(solution)/shard_map/reduce_scatter | solution.py:41
  163.8 0.9 convert_element_type.38
  164.7 3.8 %all_to_all.59 = bf16[2,16,1152]{2,1,0:T(8,128)(2,1)S(1)} all-to-all(bf16[2,16,1152]{2,1,0:T(8,128)(2,1)S(1)} %bitcast.39), channel_id=1, replica_groups=mesh['groups'=2,'dp'=2,'loop'=8] {'dp'}, dimensions={0} | all-to-all | bytes 147456 | tf_op jit(solution)/shard_map/all_to_all | solution.py:47
  168.5 0.6 copy.27
  (26 shorter events, 0.1 us)
Async XLA Ops:
  7.2 156.6 %reduce-scatter.2.cloned.1.call-start = ((), (), s32[]{:S(2)}) async-start(), calls=%async_computation.4 | async-start | bytes 1327104 | tf_op jit(solution)/shard_map/reduce_scatter | solution.py:41
  11.9 38.1 %slice-start.2 = ((s8[5308416]{0:T(1024)(128)(4,1)}), s8[4194304]{0:T(1024)(128)(4,1)S(1)}, s32[]{:S(2)}) async-start(s8[5308416]{0:T(1024)(128)(4,1)} %bitcast.48), calls=%async_computation.7 | async-start | bytes 8388608
  45.3 4.6 %copy-start.4 = (bf16[256,1152]{1,0:T(8,128)(2,1)}, bf16[256,1152]{1,0:T(8,128)(2,1)S(1)}, u32[]{:S(2)}) copy-start(bf16[256,1152]{1,0:T(8,128)(2,1)S(1)} %all_gather.7) | copy-start | bytes 1769476
  45.3 4.6 %slice-start.3 = ((s8[5308416]{0:T(1024)(128)(4,1)}), s8[1114112]{0:T(1024)(128)(4,1)S(1)}, s32[]{:S(2)}) async-start(s8[5308416]{0:T(1024)(128)(4,1)} %bitcast.48), calls=%async_computation.8 | async-start | bytes 2228224
  49.8 37.9 %slice-start = ((s8[5308416]{0:T(1024)(128)(4,1)}), s8[4194304]{0:T(1024)(128)(4,1)S(1)}, s32[]{:S(2)}) async-start(s8[5308416]{0:T(1024)(128)(4,1)} %bitcast.37), calls=%async_computation.5 | async-start | bytes 8388608
  49.9 2.4 %copy-start.6 = (bf16[16,2304]{1,0:T(8,128)(2,1)S(1)}, bf16[16,2304]{1,0:T(8,128)(2,1)}, u32[]{:S(2)}) copy-start(bf16[16,2304]{1,0:T(8,128)(2,1)} %param.6) | copy-start | bytes 221188
  49.9 37.9 %slice-start.1 = ((s8[5308416]{0:T(1024)(128)(4,1)}), s8[1114112]{0:T(1024)(128)(4,1)S(1)}, s32[]{:S(2)}) async-start(s8[5308416]{0:T(1024)(128)(4,1)} %bitcast.37), calls=%async_computation.6 | async-start | bytes 2228224
  49.9 39.7 %collective-permute-start.1 = (bf16[256,2304]{1,0:T(8,128)(2,1)S(1)}, bf16[256,2304]{1,0:T(8,128)(2,1)S(1)}, u32[]{:S(2)}, u32[]{:S(2)}) collective-permute-start(bf16[256,2304]{1,0:T(8,128)(2,1)S(1)} %get-tuple-element.26), channel_id=1, source_target_pairs={{0,8},{8,0},{1,9},{9,1},{2,10},{10,2},{3,11},{11,3},{4,12},{12,4},... | collective-permute-start | bytes 3538952 | tf_op jit(solution)/shard_map/ppermute | solution.py:34
  51.7 40.7 %copy-start = (f32[256,2304]{1,0:T(8,128)}, f32[256,2304]{1,0:T(8,128)S(1)}, u32[]{:S(2)}) copy-start(f32[256,2304]{1,0:T(8,128)S(1)} %get-tuple-element.25) | copy-start | bytes 7077892
  51.7 37.9 %collective-permute-start.2 = (bf16[256,2304]{1,0:T(8,128)(2,1)S(1)}, bf16[256,2304]{1,0:T(8,128)(2,1)S(1)}, u32[]{:S(2)}, u32[]{:S(2)}) collective-permute-start(bf16[256,2304]{1,0:T(8,128)(2,1)S(1)} %get-tuple-element.24), channel_id=1, source_target_pairs={{0,8},{8,0},{1,9},{9,1},{2,10},{10,2},{3,11},{11,3},{4,12},{12,4},... | collective-permute-start | bytes 3538952 | tf_op jit(solution)/shard_map/ppermute | solution.py:34
  87.7 1.8 copy-start.5
  87.8 8.0 %slice-start.4 = ((s8[5308416]{0:T(1024)(128)(4,1)}), s8[4194304]{0:T(1024)(128)(4,1)S(1)}, s32[]{:S(2)}) async-start(s8[5308416]{0:T(1024)(128)(4,1)} %bitcast.50), calls=%async_computation.9 | async-start | bytes 8388608
  89.5 2.9 %collective-permute-start = (bf16[256,2304]{1,0:T(8,128)(2,1)S(1)}, bf16[256,2304]{1,0:T(8,128)(2,1)S(1)}, u32[]{:S(2)}, u32[]{:S(2)}) collective-permute-start(bf16[256,2304]{1,0:T(8,128)(2,1)S(1)} %get-tuple-element.22), channel_id=1, source_target_pairs={{0,8},{8,0},{1,9},{9,1},{2,10},{10,2},{3,11},{11,3},{4,12},{12,4},... | collective-permute-start | bytes 3538952 | tf_op jit(solution)/shard_map/ppermute | solution.py:34
  89.6 4.3 %copy-start.1 = (bf16[256,2304]{1,0:T(8,128)(2,1)}, bf16[256,2304]{1,0:T(8,128)(2,1)S(1)}, u32[]{:S(2)}) copy-start(bf16[256,2304]{1,0:T(8,128)(2,1)S(1)} %collective-permute-done.2) | copy-start | bytes 3538948
  92.4 3.3 %slice-start.5 = ((s8[5308416]{0:T(1024)(128)(4,1)}), s8[1114112]{0:T(1024)(128)(4,1)S(1)}, s32[]{:S(2)}) async-start(s8[5308416]{0:T(1024)(128)(4,1)} %bitcast.50), calls=%async_computation.10 | async-start | bytes 2228224
  94.0 1.7 copy-start.3
  94.0 1.7 copy-start.2
Sparse Core Ops, SparseCore 0:
  98.7 65.0 reduce-scatter.1
where the time goes:
time: 177 us; the launch traced here: 176 us
  blocking collectives  76.4 us (43%)
  matrix products  35.5 us (20%)
  local copies, waits for them, and re-layouts  27 us (15%)
  waiting for transfers between devices  19.5 us (11%)
  between operations  14.3 us (8%)
  other arithmetic  2.45 us (1%)
    all_gather x2, blocking collectives, halves(): return lax.all_gather(rows, 'loop', axis=0, tiled=True)  65.2 us
    unnamed x28, local copies, waits for them, and re-layouts  25.5 us
    dot_general x3, matrix products, contract_first(): lax.dot_general(left, right, (((0,), (0,)), ((), ())), preferred_element_...  23.1 us
    reduce_scatter x1, waiting for transfers between devices, on_device(): lax.psum_scatter(contract_last(grad_gate_pre, gate_weight) + contract_las...  16.7 us
    all_to_all x2, blocking collectives, halves(): rows = lax.all_to_all(rows, 'dp', split_axis=1, concat_axis=0, tiled=True)  7.51 us
    dot_general x3, matrix products, contract_last(): lax.dot_general(left, right, (((1,), (1,)), ((), ())), preferred_element_...  6.2 us
    dot_general x1, matrix products, on_device(): up = both(jnp.dot(features, up_weight, preferred_element_type=jnp.float32))  4.49 us
    all_to_all x1, blocking collectives, on_device(): lax.all_to_all(grad_rows, 'dp', split_axis=0, concat_axis=1, tiled=True)  3.76 us
  transfers between devices with their start and end apart: 4, of which 2 were waited for; matrix products, arithmetic and copies ran while one was open for 30% of the time, Pallas kernels for 0%

commit v1 on v0

v1 whole, which is shorter than its diff:
```python
import functools

import jax
import jax.numpy as jnp
from jax import lax
from jax.experimental import pallas as pl
from jax.experimental.pallas import tpu as pltpu
from jax.sharding import PartitionSpec as P

MESH = pl.DeviceIdType.MESH
MIB = 1024 * 1024


def contract_last(left, right):
    return lax.dot_general(
        left, right, (((1,), (1,)), ((), ())), preferred_element_type=jnp.float32
    )


def contract_first(left, right):
    return lax.dot_general(
        left, right, (((0,), (0,)), ((), ())), preferred_element_type=jnp.float32
    )


def pointwise(gate, up, grad_hidden):
    sigma = jax.nn.sigmoid(gate)
    hidden = (gate * sigma * up).astype(jnp.bfloat16)
    grad_gate_pre = (grad_hidden * up * (sigma + gate * sigma * (1.0 - sigma))).astype(jnp.bfloat16)
    grad_up_pre = (grad_hidden * gate * sigma).astype(jnp.bfloat16)
    return (hidden, grad_gate_pre, grad_up_pre)


def hidden_kernel(
    loop, width, chunks,
    tokens, grad_out, gate_w, up_w, down_w,
    features, upstream, hidden, grad_gate_pre, grad_up_pre, terms,
    held, gate_v, up_v, down_v, own, sent, got, total,
    load_sem, half_send, half_recv, ring_send, ring_recv, part_send, part_recv,
):
    g, c, l = lax.axis_index("groups"), lax.axis_index("dp"), lax.axis_index("loop")
    depth = loop // width
    z, y = l // width, l % width
    rows, half = tokens.shape[0], gate_w.shape[0]
    chunk = gate_v.shape[2]
    count = loop * 2 * rows

    def load(k, i):
        cols = pl.ds(i * chunk, chunk)
        source = down_w.at[cols] if k == 2 else (gate_w, up_w)[k].at[:, cols]
        return pltpu.make_async_copy(source, (gate_v, up_v, down_v)[k].at[i], load_sem.at[k, i])

    barrier = pltpu.get_barrier_semaphore()

    def greet(device):
        pl.semaphore_signal(barrier, inc=1, device_id=device, device_id_type=MESH)

    greet((g, 1 - c, l))
    if width == 2:
        greet((g, c, z * width + 1 - y))
    pl.when(z > 0)(lambda: greet((g, c, l - width)))
    pl.when(z < depth - 1)(lambda: greet((g, c, l + width)))
    inner = jnp.where(z > 0, 1, 0) + jnp.where(z < depth - 1, 1, 0)
    for k in range(3):
        for i in range(chunks):
            load(k, i).start()
    pl.semaphore_wait(barrier, (2 if width == 2 else 1) + inner)

    mine = pl.ds(pl.multiple_of(c * rows, rows), rows)
    kept = pl.ds(pl.multiple_of(c * half, 128), half)
    given = pl.ds(pl.multiple_of((1 - c) * half, 128), half)

    def swap(a):
        ref = (tokens, grad_out)[a]
        return pltpu.make_async_remote_copy(
            src_ref=ref.at[:, given], dst_ref=held.at[a, l, mine],
            send_sem=half_send.at[a], recv_sem=half_recv.at[a],
            device_id=(g, 1 - c, l), device_id_type=MESH,
        )

    for a in range(2):
        swap(a).start()
    for a in range(2):
        held[a, l, mine, :] = (tokens, grad_out)[a][:, kept]

    def move(a, block, way):
        target = (l + width, l - width, z * width + 1 - y)[way]
        return pltpu.make_async_remote_copy(
            src_ref=held.at[a, block], dst_ref=held.at[a, block],
            send_sem=ring_send.at[a, block, way], recv_sem=ring_recv.at[a, block],
            device_id=(g, c, target), device_id_type=MESH,
        )

    def sends(a, d, act):
        def from_below():
            block = l - d * width
            if act == "start" and d:
                move(a, block, 0).wait_recv()
            pl.when(z < depth - 1)(lambda: getattr(move(a, block, 0), act)())
            if width == 2:
                getattr(move(a, block, 2), act)()

        def from_above():
            block = l + d * width
            if act == "start" and d:
                move(a, block, 1).wait_recv()
            pl.when(z > 0)(lambda: getattr(move(a, block, 1), act)())
            if width == 2 and d:
                getattr(move(a, block, 2), act)()

        if d == 0:
            if act == "start":
                swap(a).wait_recv()
            from_below()
            from_above()
        else:
            pl.when(z - d >= 0)(from_below)
            pl.when(z + d < depth)(from_above)

    def across(a):
        if width == 2:
            for k in range(depth):
                move(a, k * width + 1 - y, 2).wait_recv()

    sends(0, 0, "start")
    for d in range(1, depth):
        sends(0, d, "start")
        sends(1, d - 1, "start")
    across(0)

    def part(k, i):
        return pltpu.make_async_remote_copy(
            src_ref=sent.at[k, i], dst_ref=got.at[k, i],
            send_sem=part_send.at[k, i], recv_sem=part_recv.at[k, i],
            device_id=(g, 1 - c, l), device_id_type=MESH,
        )

    def forward(k):
        def step(i, carry):
            load(k, i).wait()
            x = held[min(1, k // 2)].reshape(count, half)
            if k == 2:
                term = contract_last(x, down_v[i])
            else:
                term = jnp.dot(x, (gate_v, up_v)[k][i], preferred_element_type=jnp.float32)
            own[k, i] = term
            sent[k, i] = term.astype(jnp.bfloat16)
            part(k, i).start()
            return carry

        lax.fori_loop(0, chunks, step, 0)

    forward(0)
    sends(1, depth - 1, "start")
    forward(1)
    across(1)
    forward(2)
    for a, out in enumerate((features, upstream)):
        out[...] = held[a].reshape(count, half)
    total[...] = jnp.zeros_like(total)

    def back(i, carry):
        whole = []
        for k in range(3):
            part(k, i).wait_recv()
            whole.append(own[k, i] + got[k, i].astype(jnp.float32))
        h, gg, gu = pointwise(*whole)
        cols = pl.ds(pl.multiple_of(i * chunk, chunk), chunk)
        hidden[:, cols] = h
        grad_gate_pre[:, cols] = gg
        grad_up_pre[:, cols] = gu
        total[...] += contract_last(gg, gate_v[i]) + contract_last(gu, up_v[i])
        return carry

    lax.fori_loop(0, chunks, back, 0)
    for k in range(loop):
        to = lax.rem(l + k, loop) * 2
        for e in range(2):
            at = to + (c if e == 0 else 1 - c)
            terms[e, k] = total[pl.ds(pl.multiple_of(at * rows, rows), rows), :].astype(jnp.bfloat16)

    def drain(i, carry):
        for k in range(3):
            part(k, i).wait_send()
        return carry

    lax.fori_loop(0, chunks, drain, 0)
    for a in range(2):
        swap(a).wait_send()
        for d in range(depth):
            sends(a, d, "wait_send")


def find_hidden(loop, width, tokens, grad_out, gate_weight, up_weight, down_weight):
    rows = tokens.shape[0]
    half, units = gate_weight.shape
    count = loop * 2 * rows
    chunk = next((n for n in (384, 256, 128) if units % n == 0), units)
    chunks = units // chunk
    bf16, f32 = jnp.bfloat16, jnp.float32
    vmem, far = pl.BlockSpec(memory_space=pltpu.VMEM), pl.BlockSpec(memory_space=pl.ANY)
    dma = pltpu.SemaphoreType.DMA
    return pl.pallas_call(
        functools.partial(hidden_kernel, loop, width, chunks),
        out_shape=[jax.ShapeDtypeStruct((count, half), bf16)] * 2
        + [jax.ShapeDtypeStruct((count, units), bf16)] * 3
        + [jax.ShapeDtypeStruct((2, loop, rows, half), bf16)],
        in_specs=[vmem, vmem, far, far, far],
        out_specs=[vmem] * 6,
        scratch_shapes=[
            pltpu.VMEM((2, loop, 2 * rows, half), bf16),
            pltpu.VMEM((chunks, half, chunk), bf16),
            pltpu.VMEM((chunks, half, chunk), bf16),
            pltpu.VMEM((chunks, chunk, half), bf16),
            pltpu.VMEM((3, chunks, count, chunk), f32),
            pltpu.VMEM((3, chunks, count, chunk), bf16),
            pltpu.VMEM((3, chunks, count, chunk), bf16),
            pltpu.VMEM((count, half), f32),
            dma((3, chunks)), dma((2,)), dma((2,)),
            dma((2, loop, 3)), dma((2, loop)), dma((3, chunks)), dma((3, chunks)),
        ],
        compiler_params=pltpu.CompilerParams(
            collective_id=0, has_side_effects=True, vmem_limit_bytes=58 * MIB
        ),
        cost_estimate=pl.CostEstimate(
            flops=10 * count * half * units,
            bytes_accessed=6 * half * units + 10 * count * (units + half),
            transcendentals=count * units,
        ),
        name="find_hidden",
    )(tokens, grad_out, gate_weight, up_weight, down_weight)


def gradient_kernel(features, grad_gate_pre, grad_up_pre, hidden, upstream, gate, up, down):
    gate[...] = contract_first(features[...], grad_gate_pre[...])
    up[...] = contract_first(features[...], grad_up_pre[...])
    down[...] = contract_first(hidden[...], upstream[...])


def weight_gradients(features, upstream, hidden, grad_gate_pre, grad_up_pre):
    count, half = features.shape
    units = hidden.shape[1]
    steps = half // 128
    if half % 128 or units % (128 * steps):
        return (
            contract_first(features, grad_gate_pre),
            contract_first(features, grad_up_pre),
            contract_first(hidden, upstream),
        )
    whole = lambda cols: pl.BlockSpec((count, cols), lambda i: (0, 0))
    slab = lambda cols: pl.BlockSpec((count, cols), lambda i: (0, i))
    rows = lambda n, cols: pl.BlockSpec((n, cols), lambda i: (i, 0))
    tall, wide = half // steps, units // steps
    return pl.pallas_call(
        gradient_kernel,
        grid=(steps,),
        out_shape=[jax.ShapeDtypeStruct((half, units), jnp.float32)] * 2
        + [jax.ShapeDtypeStruct((units, half), jnp.float32)],
        in_specs=[slab(tall), whole(units), whole(units), slab(wide), whole(half)],
        out_specs=[rows(tall, units), rows(tall, units), rows(wide, half)],
        compiler_params=pltpu.CompilerParams(vmem_limit_bytes=40 * MIB),
        cost_estimate=pl.CostEstimate(
            flops=6 * count * half * units,
            bytes_accessed=12 * half * units + 2 * count * (3 * units + 2 * half),
            transcendentals=0,
        ),
        name="weight_gradients",
    )(features, grad_gate_pre, grad_up_pre, hidden, upstream)


def sum_terms(loop, terms):
    halves = []
    for e in range(2):
        total = None
        for k in range(loop):
            term = terms[e, k]
            if e or k:
                pairs = [
                    (c * loop + l, (c ^ e) * loop + (l + k) % loop)
                    for c in range(2)
                    for l in range(loop)
                ]
                term = lax.ppermute(term, ("dp", "loop"), pairs)
            term = term.astype(jnp.float32)
            total = term if total is None else total + term
        halves.append(total)
    kept, other = halves
    first = lax.axis_index("dp") == 0
    low, high = jnp.where(first, kept, other), jnp.where(first, other, kept)
    return jnp.concatenate([low, high], axis=1).astype(jnp.bfloat16)


def on_device(loop, width, tokens, grad_out, gate_weight, up_weight, down_weight):
    features, upstream, hidden, grad_gate_pre, grad_up_pre, terms = find_hidden(
        loop, width, tokens, grad_out, gate_weight, up_weight, down_weight
    )
    grad_gate, grad_up, grad_down = weight_gradients(
        features, upstream, hidden, grad_gate_pre, grad_up_pre
    )
    return (sum_terms(loop, terms), grad_gate, grad_up, grad_down)


def columns(mesh):
    line = mesh.devices[0, 0]
    z = [getattr(device, "coords", (0, 0, k // 2))[2] for k, device in enumerate(line)]
    side = sum(n == z[0] for n in z)
    return 2 if side == 2 and len(z) % 2 == 0 else 1


def solution(mesh):
    in_specs = (
        P(("groups", "dp", "loop"), None),
        P(("groups", "dp", "loop"), None),
        P("dp", "loop"),
        P("dp", "loop"),
        P("loop", "dp"),
    )
    out_specs = (
        P(("groups", "dp", "loop"), None),
        P(("groups", "dp"), "loop"),
        P(("groups", "dp"), "loop"),
        P(("groups", "loop"), "dp"),
    )
    return jax.shard_map(
        functools.partial(on_device, mesh.shape["loop"], columns(mesh)),
        mesh=mesh, in_specs=in_specs, out_specs=out_specs, check_vma=False,
    )
```

time: 177 us -> 79.6 us (0.45)
  blocking collectives: 76.4 us -> 0 us
  Pallas kernels: 0 us -> 51.4 us
  matrix products: 35.5 us -> 0 us
  local copies, waits for them, and re-layouts: 27 us -> 7.01 us
  waiting for transfers between devices: 19.5 us -> 0.04 us
  starting transfers between devices: 0.72 us -> 18.5 us
  between operations: 14.3 us -> 0.7 us
    all_gather x2 -> x0, blocking collectives: 65.2 us -> none  [halves(): return lax.all_gather(rows, 'loop', axis=0, tiled=True)]
    pallas_call x0 -> x2, Pallas kernels: none -> 51.4 us  [the longest x1 40.6 us: find_hidden(): pl.pallas_call(functools.partial(hidden_kernel, loop, width, chunks), out...]
    dot_general x8 -> x0, matrix products: 35.5 us -> none  [the longest x3 23.1 us: contract_first(): lax.dot_general(left, right, (((0,), (0,)), ((), ())), preferred_element_...]
    unnamed x28 -> x10, local copies, waits for them, and re-layouts: 25.5 us -> 5.94 us
    ppermute x3 -> x15, starting transfers between devices: 0.68 us -> 18.5 us  [sum_terms(): term = lax.ppermute(term, ('dp', 'loop'), pairs)]
    reduce_scatter x1 -> x0, waiting for transfers between devices: 16.7 us -> none  [on_device(): lax.psum_scatter(contract_last(grad_gate_pre, gate_weight) + contract_las...]
    all_to_all x3 -> x0, blocking collectives: 11.3 us -> none  [the longest x2 7.51 us: halves(): rows = lax.all_to_all(rows, 'dp', split_axis=1, concat_axis=0, tiled=True)]
    ppermute x3 -> x15, waiting for transfers between devices: 2.81 us -> 0.04 us  [sum_terms(): term = lax.ppermute(term, ('dp', 'loop'), pairs)]
  transfers between devices with their start and end apart: 4 -> 15, of which waited for: 2 -> 0; matrix products, arithmetic and copies ran while one was open for 30% -> 0% of each run, Pallas kernels for 0% -> 14%
where the time goes in v1:
time: 79.6 us; the launch traced here: 79.1 us
  Pallas kernels  51.4 us (65%)
  starting transfers between devices  18.5 us (23%)
  local copies, waits for them, and re-layouts  7.01 us (9%)
  other arithmetic  1.51 us (2%)
    pallas_call x1, Pallas kernels, find_hidden(): pl.pallas_call(functools.partial(hidden_kernel, loop, width, chunks), out...  40.6 us
    ppermute x15, starting transfers between devices, sum_terms(): term = lax.ppermute(term, ('dp', 'loop'), pairs)  18.5 us
    pallas_call x1, Pallas kernels, weight_gradients(): pl.pallas_call(gradient_kernel, grid=(steps,), out_shape=[jax.ShapeDtypeS...  10.8 us
    unnamed x10, local copies, waits for them, and re-layouts  5.94 us
  transfers between devices with their start and end apart: 15, of which 0 were waited for; matrix products, arithmetic and copies ran while one was open for 0% of the time, Pallas kernels for 14%

profile of v1, /device:TPU:0, one launch (start us, length us, event | category | flops | bytes accessed | tf_op | source)
XLA Modules:
  0.0 79.1 jit_solution(11113610861352884535)
XLA Ops:
  0.6 40.6 %find_hidden.1 = (bf16[256,1152]{1,0:T(8,128)(2,1)}, bf16[256,1152]{1,0:T(8,128)(2,1)}, bf16[256,2304]{1,0:T(8,128)(2,1)}, bf16[256,2304]{1,0:T(8,128)(2,1)}, bf...) custom-call(bf16[16,2304]{1,0:T(8,128)(2,1)} %tokens.1, bf16[16,2304]{1,0:T(8,128)(2,1)} %grad_out.1, ...), custom_call_target="tpu_custom_call" | custom-call | flops 6794772480 | bytes 24772608 | tf_op jit(solution)/shard_map/find_hidden/pallas_call | solution.py:203
  41.2 1.1 %slice_bitcast_fusion.7 = (bf16[16,1152]{1,0:T(8,128)(2,1)S(1)}, bf16[16,1152]{1,0:T(8,128)(2,1)S(1)}, bf16[16,1152]{1,0:T(8,128)(2,1)S(1)}, bf16[16,1152]{1,0:T...) fusion(bf16[2,8,16,1152]{3,2,1,0:T(8,128)(2,1)} %get-tuple-elem, ...), kind=kLoop, calls=%fused_computation.18 | loop fusion | bytes 1105920 | tf_op jit(solution)/shard_map/squeeze | solution.py:276
  42.3 0.1 collective-permute-start.7
  42.4 1.7 %collective-permute-start.14 = (bf16[16,1152]{1,0:T(8,128)(2,1)S(1)}, bf16[16,1152]{1,0:T(8,128)(2,1)S(1)}, u32[]{:S(2)}, u32[]{:S(2)}) collective-permute-start(bf16[16,1152]{1,0:T(8,128)(2,1)S(1)} %get-tuple-element.26), channel_id=1, source_target_pairs={{0,15},{1,8},{2,9},{3,10},{4,11},{5,12},{6,13},{7,14},{8,7},{9,0},... | collective-permute-start | bytes 110600 | tf_op jit(solution)/shard_map/ppermute | solution.py:283
  44.1 0.0 collective-permute-start.13
  44.1 0.0 collective-permute-start.12
  44.1 2.9 %collective-permute-start.11 = (bf16[16,1152]{1,0:T(8,128)(2,1)S(1)}, bf16[16,1152]{1,0:T(8,128)(2,1)S(1)}, u32[]{:S(2)}, u32[]{:S(2)}) collective-permute-start(bf16[16,1152]{1,0:T(8,128)(2,1)S(1)} %get-tuple-element.29), channel_id=1, source_target_pairs={{0,12},{1,13},{2,14},{3,15},{4,8},{5,9},{6,10},{7,11},{8,4},{9,5},... | collective-permute-start | bytes 110600 | tf_op jit(solution)/shard_map/ppermute | solution.py:283
  46.9 0.0 collective-permute-done.7
  47.0 1.4 %collective-permute-start.10 = (bf16[16,1152]{1,0:T(8,128)(2,1)S(1)}, bf16[16,1152]{1,0:T(8,128)(2,1)S(1)}, u32[]{:S(2)}, u32[]{:S(2)}) collective-permute-start(bf16[16,1152]{1,0:T(8,128)(2,1)S(1)} %get-tuple-element.30), channel_id=1, source_target_pairs={{0,11},{1,12},{2,13},{3,14},{4,15},{5,8},{6,9},{7,10},{8,3},{9,4},... | collective-permute-start | bytes 110600 | tf_op jit(solution)/shard_map/ppermute | solution.py:283
  48.4 0.0 collective-permute-done.14
  48.4 0.1 collective-permute-start.9
  48.5 0.0 collective-permute-done.13
  48.5 1.1 %collective-permute-start.8 = (bf16[16,1152]{1,0:T(8,128)(2,1)S(1)}, bf16[16,1152]{1,0:T(8,128)(2,1)S(1)}, u32[]{:S(2)}, u32[]{:S(2)}) collective-permute-start(bf16[16,1152]{1,0:T(8,128)(2,1)S(1)} %get-tuple-element.32), channel_id=1, source_target_pairs={{0,9},{1,10},{2,11},{3,12},{4,13},{5,14},{6,15},{7,8},{8,1},{9,2},... | collective-permute-start | bytes 110600 | tf_op jit(solution)/shard_map/ppermute | solution.py:283
  49.6 3.3 %collective-permute-start.6 = (bf16[16,1152]{1,0:T(8,128)(2,1)S(1)}, bf16[16,1152]{1,0:T(8,128)(2,1)S(1)}, u32[]{:S(2)}, u32[]{:S(2)}) collective-permute-start(bf16[16,1152]{1,0:T(8,128)(2,1)S(1)} %get-tuple-element.33), channel_id=1, source_target_pairs={{0,7},{1,0},{2,1},{3,2},{4,3},{5,4},{6,5},{7,6},{8,15},{9,8},{10,9... | collective-permute-start | bytes 110600 | tf_op jit(solution)/shard_map/ppermute | solution.py:283
  52.9 2.0 %collective-permute-start.5 = (bf16[16,1152]{1,0:T(8,128)(2,1)S(1)}, bf16[16,1152]{1,0:T(8,128)(2,1)S(1)}, u32[]{:S(2)}, u32[]{:S(2)}) collective-permute-start(bf16[16,1152]{1,0:T(8,128)(2,1)S(1)} %get-tuple-element.34), channel_id=1, source_target_pairs={{0,6},{1,7},{2,0},{3,1},{4,2},{5,3},{6,4},{7,5},{8,14},{9,15},{10,... | collective-permute-start | bytes 110600 | tf_op jit(solution)/shard_map/ppermute | solution.py:283
  54.9 0.1 collective-permute-start.4
  55.0 1.8 %collective-permute-start.3 = (bf16[16,1152]{1,0:T(8,128)(2,1)S(1)}, bf16[16,1152]{1,0:T(8,128)(2,1)S(1)}, u32[]{:S(2)}, u32[]{:S(2)}) collective-permute-start(bf16[16,1152]{1,0:T(8,128)(2,1)S(1)} %get-tuple-element.36), channel_id=1, source_target_pairs={{0,4},{1,5},{2,6},{3,7},{4,0},{5,1},{6,2},{7,3},{8,12},{9,13},{10,... | collective-permute-start | bytes 110600 | tf_op jit(solution)/shard_map/ppermute | solution.py:283
  56.9 0.0 collective-permute-done.8
  56.9 1.1 %collective-permute-start.2 = (bf16[16,1152]{1,0:T(8,128)(2,1)S(1)}, bf16[16,1152]{1,0:T(8,128)(2,1)S(1)}, u32[]{:S(2)}, u32[]{:S(2)}) collective-permute-start(bf16[16,1152]{1,0:T(8,128)(2,1)S(1)} %get-tuple-element.37), channel_id=1, source_target_pairs={{0,3},{1,4},{2,5},{3,6},{4,7},{5,0},{6,1},{7,2},{8,11},{9,12},{10,... | collective-permute-start | bytes 110600 | tf_op jit(solution)/shard_map/ppermute | solution.py:283
  57.9 2.9 %collective-permute-start.1 = (bf16[16,1152]{1,0:T(8,128)(2,1)S(1)}, bf16[16,1152]{1,0:T(8,128)(2,1)S(1)}, u32[]{:S(2)}, u32[]{:S(2)}) collective-permute-start(bf16[16,1152]{1,0:T(8,128)(2,1)S(1)} %get-tuple-element.38), channel_id=1, source_target_pairs={{0,2},{1,3},{2,4},{3,5},{4,6},{5,7},{6,0},{7,1},{8,10},{9,11},{10,... | collective-permute-start | bytes 110600 | tf_op jit(solution)/shard_map/ppermute | solution.py:283
  60.8 0.0 collective-permute-done.5
  60.8 1.3 %copy-done = bf16[256,2304]{1,0:T(8,128)(2,1)S(1)} copy-done((bf16[256,2304]{1,0:T(8,128)(2,1)S(1)}, bf16[256,2304]{1,0:T(8,128)(2,1)}, u32[]{:S(2)}) %copy-start) | copy-done | bytes 1179672
  62.1 1.3 %copy-done.1 = bf16[256,2304]{1,0:T(8,128)(2,1)S(1)} copy-done((bf16[256,2304]{1,0:T(8,128)(2,1)S(1)}, bf16[256,2304]{1,0:T(8,128)(2,1)}, u32[]{:S(2)}) %copy-start.1) | copy-done | bytes 1179672
  63.4 1.3 %copy-done.2 = bf16[256,2304]{1,0:T(8,128)(2,1)S(1)} copy-done((bf16[256,2304]{1,0:T(8,128)(2,1)S(1)}, bf16[256,2304]{1,0:T(8,128)(2,1)}, u32[]{:S(2)}) %copy-start.2) | copy-done | bytes 1179672
  64.6 1.1 %copy-done.3 = bf16[256,1152]{1,0:T(8,128)(2,1)S(1)} copy-done((bf16[256,1152]{1,0:T(8,128)(2,1)S(1)}, bf16[256,1152]{1,0:T(8,128)(2,1)}, u32[]{:S(2)}) %copy-start.3) | copy-done | bytes 589848
  65.7 1.1 %copy-done.4 = bf16[256,1152]{1,0:T(8,128)(2,1)S(1)} copy-done((bf16[256,1152]{1,0:T(8,128)(2,1)S(1)}, bf16[256,1152]{1,0:T(8,128)(2,1)}, u32[]{:S(2)}) %copy-start.4) | copy-done | bytes 589848
  66.8 10.8 %weight_gradients.1 = (f32[1152,2304]{1,0:T(8,128)}, f32[1152,2304]{1,0:T(8,128)}, f32[2304,1152]{1,0:T(8,128)}) custom-call(bf16[256,1152]{1,0:T(8,128)(2,1)S(1)} %copy-done.3, bf16[256,2304]{1,0:T(8,128)(2,1)S(1)} %copy-done.1, bf16[256,2304]{1,0:T(8,128)(2,1)S(1)} %copy-done.2, bf16[256,2304]{1,0:T(8,128)(2,1)S(1)} %copy-done, bf16[256,1152]{1,0:T(8,128)(2,1)S(1)} %copy-done.4), custom_call_target="tpu_custom_call" | custom-call | flops 4076863488 | bytes 36569088 | tf_op jit(solution)/shard_map/weight_gradients/pallas_call | solution.py:254
  77.6 0.0 collective-permute-done.4
  77.6 0.0 collective-permute-done.3
  77.6 0.0 collective-permute-done.1
  77.6 0.9 %select_convert_fusion.1 = (bf16[16,1152]{1,0:T(8,128)(2,1)S(1)}, bf16[16,1152]{1,0:T(8,128)(2,1)S(1)}, bf16[16,1152]{1,0:T(8,128)(2,1)S(1)}) fusion(pred[]{:T(512)S(6)} %eq.3, bf16[16,1152]{1,0:T(8,128)(2,1)S(1)} %collective-permute-done.6, bf16[16,1152]{1,0:T(8,128)(2,1)S(1)} %collective-permute-done.5, bf16[16,1152]{1,0:T(8,128)(2,1)S(1)} %collective-permute-done.4, ...), kind=kLoop, calls=%fused_computation.9 | loop fusion | flops 608256 | bytes 700417 | tf_op jit(solution)/shard_map/convert.1
  78.5 0.6 pad_maximum_fusion
  (14 shorter events, 0.0 us)
Async XLA Ops:
  42.3 4.7 %collective-permute-start.7 = (bf16[16,1152]{1,0:T(8,128)(2,1)S(1)}, bf16[16,1152]{1,0:T(8,128)(2,1)S(1)}, u32[]{:S(2)}, u32[]{:S(2)}) collective-permute-start(bf16[16,1152]{1,0:T(8,128)(2,1)S(1)} %get-tuple-element.25), channel_id=1, source_target_pairs={{0,8},{1,9},{2,10},{3,11},{4,12},{5,13},{6,14},{7,15},{8,0},{9,1},... | collective-permute-start | bytes 110600 | tf_op jit(solution)/shard_map/ppermute | solution.py:283
  42.4 6.0 %collective-permute-start.14 = (bf16[16,1152]{1,0:T(8,128)(2,1)S(1)}, bf16[16,1152]{1,0:T(8,128)(2,1)S(1)}, u32[]{:S(2)}, u32[]{:S(2)}) collective-permute-start(bf16[16,1152]{1,0:T(8,128)(2,1)S(1)} %get-tuple-element.26), channel_id=1, source_target_pairs={{0,15},{1,8},{2,9},{3,10},{4,11},{5,12},{6,13},{7,14},{8,7},{9,0},... | collective-permute-start | bytes 110600 | tf_op jit(solution)/shard_map/ppermute | solution.py:283
  44.1 4.4 %collective-permute-start.13 = (bf16[16,1152]{1,0:T(8,128)(2,1)S(1)}, bf16[16,1152]{1,0:T(8,128)(2,1)S(1)}, u32[]{:S(2)}, u32[]{:S(2)}) collective-permute-start(bf16[16,1152]{1,0:T(8,128)(2,1)S(1)} %get-tuple-element.27), channel_id=1, source_target_pairs={{0,14},{1,15},{2,8},{3,9},{4,10},{5,11},{6,12},{7,13},{8,6},{9,7},... | collective-permute-start | bytes 110600 | tf_op jit(solution)/shard_map/ppermute | solution.py:283
  44.1 5.5 %collective-permute-start.12 = (bf16[16,1152]{1,0:T(8,128)(2,1)S(1)}, bf16[16,1152]{1,0:T(8,128)(2,1)S(1)}, u32[]{:S(2)}, u32[]{:S(2)}) collective-permute-start(bf16[16,1152]{1,0:T(8,128)(2,1)S(1)} %get-tuple-element.28), channel_id=1, source_target_pairs={{0,13},{1,14},{2,15},{3,8},{4,9},{5,10},{6,11},{7,12},{8,5},{9,6},... | collective-permute-start | bytes 110600 | tf_op jit(solution)/shard_map/ppermute | solution.py:283
  44.1 8.8 %collective-permute-start.11 = (bf16[16,1152]{1,0:T(8,128)(2,1)S(1)}, bf16[16,1152]{1,0:T(8,128)(2,1)S(1)}, u32[]{:S(2)}, u32[]{:S(2)}) collective-permute-start(bf16[16,1152]{1,0:T(8,128)(2,1)S(1)} %get-tuple-element.29), channel_id=1, source_target_pairs={{0,12},{1,13},{2,14},{3,15},{4,8},{5,9},{6,10},{7,11},{8,4},{9,5},... | collective-permute-start | bytes 110600 | tf_op jit(solution)/shard_map/ppermute | solution.py:283
  47.0 7.9 %collective-permute-start.10 = (bf16[16,1152]{1,0:T(8,128)(2,1)S(1)}, bf16[16,1152]{1,0:T(8,128)(2,1)S(1)}, u32[]{:S(2)}, u32[]{:S(2)}) collective-permute-start(bf16[16,1152]{1,0:T(8,128)(2,1)S(1)} %get-tuple-element.30), channel_id=1, source_target_pairs={{0,11},{1,12},{2,13},{3,14},{4,15},{5,8},{6,9},{7,10},{8,3},{9,4},... | collective-permute-start | bytes 110600 | tf_op jit(solution)/shard_map/ppermute | solution.py:283
  48.4 6.6 %collective-permute-start.9 = (bf16[16,1152]{1,0:T(8,128)(2,1)S(1)}, bf16[16,1152]{1,0:T(8,128)(2,1)S(1)}, u32[]{:S(2)}, u32[]{:S(2)}) collective-permute-start(bf16[16,1152]{1,0:T(8,128)(2,1)S(1)} %get-tuple-element.31), channel_id=1, source_target_pairs={{0,10},{1,11},{2,12},{3,13},{4,14},{5,15},{6,8},{7,9},{8,2},{9,3},... | collective-permute-start | bytes 110600 | tf_op jit(solution)/shard_map/ppermute | solution.py:283
  48.5 8.4 %collective-permute-start.8 = (bf16[16,1152]{1,0:T(8,128)(2,1)S(1)}, bf16[16,1152]{1,0:T(8,128)(2,1)S(1)}, u32[]{:S(2)}, u32[]{:S(2)}) collective-permute-start(bf16[16,1152]{1,0:T(8,128)(2,1)S(1)} %get-tuple-element.32), channel_id=1, source_target_pairs={{0,9},{1,10},{2,11},{3,12},{4,13},{5,14},{6,15},{7,8},{8,1},{9,2},... | collective-permute-start | bytes 110600 | tf_op jit(solution)/shard_map/ppermute | solution.py:283
  49.6 8.3 %collective-permute-start.6 = (bf16[16,1152]{1,0:T(8,128)(2,1)S(1)}, bf16[16,1152]{1,0:T(8,128)(2,1)S(1)}, u32[]{:S(2)}, u32[]{:S(2)}) collective-permute-start(bf16[16,1152]{1,0:T(8,128)(2,1)S(1)} %get-tuple-element.33), channel_id=1, source_target_pairs={{0,7},{1,0},{2,1},{3,2},{4,3},{5,4},{6,5},{7,6},{8,15},{9,8},{10,9... | collective-permute-start | bytes 110600 | tf_op jit(solution)/shard_map/ppermute | solution.py:283
  52.9 7.9 %collective-permute-start.5 = (bf16[16,1152]{1,0:T(8,128)(2,1)S(1)}, bf16[16,1152]{1,0:T(8,128)(2,1)S(1)}, u32[]{:S(2)}, u32[]{:S(2)}) collective-permute-start(bf16[16,1152]{1,0:T(8,128)(2,1)S(1)} %get-tuple-element.34), channel_id=1, source_target_pairs={{0,6},{1,7},{2,0},{3,1},{4,2},{5,3},{6,4},{7,5},{8,14},{9,15},{10,... | collective-permute-start | bytes 110600 | tf_op jit(solution)/shard_map/ppermute | solution.py:283
  54.9 22.7 %collective-permute-start.4 = (bf16[16,1152]{1,0:T(8,128)(2,1)S(1)}, bf16[16,1152]{1,0:T(8,128)(2,1)S(1)}, u32[]{:S(2)}, u32[]{:S(2)}) collective-permute-start(bf16[16,1152]{1,0:T(8,128)(2,1)S(1)} %get-tuple-element.35), channel_id=1, source_target_pairs={{0,5},{1,6},{2,7},{3,0},{4,1},{5,2},{6,3},{7,4},{8,13},{9,14},{10,... | collective-permute-start | bytes 110600 | tf_op jit(solution)/shard_map/ppermute | solution.py:283
  55.0 22.6 %collective-permute-start.3 = (bf16[16,1152]{1,0:T(8,128)(2,1)S(1)}, bf16[16,1152]{1,0:T(8,128)(2,1)S(1)}, u32[]{:S(2)}, u32[]{:S(2)}) collective-permute-start(bf16[16,1152]{1,0:T(8,128)(2,1)S(1)} %get-tuple-element.36), channel_id=1, source_target_pairs={{0,4},{1,5},{2,6},{3,7},{4,0},{5,1},{6,2},{7,3},{8,12},{9,13},{10,... | collective-permute-start | bytes 110600 | tf_op jit(solution)/shard_map/ppermute | solution.py:283
  56.9 20.7 %collective-permute-start.2 = (bf16[16,1152]{1,0:T(8,128)(2,1)S(1)}, bf16[16,1152]{1,0:T(8,128)(2,1)S(1)}, u32[]{:S(2)}, u32[]{:S(2)}) collective-permute-start(bf16[16,1152]{1,0:T(8,128)(2,1)S(1)} %get-tuple-element.37), channel_id=1, source_target_pairs={{0,3},{1,4},{2,5},{3,6},{4,7},{5,0},{6,1},{7,2},{8,11},{9,12},{10,... | collective-permute-start | bytes 110600 | tf_op jit(solution)/shard_map/ppermute | solution.py:283
  57.9 19.6 %collective-permute-start.1 = (bf16[16,1152]{1,0:T(8,128)(2,1)S(1)}, bf16[16,1152]{1,0:T(8,128)(2,1)S(1)}, u32[]{:S(2)}, u32[]{:S(2)}) collective-permute-start(bf16[16,1152]{1,0:T(8,128)(2,1)S(1)} %get-tuple-element.38), channel_id=1, source_target_pairs={{0,2},{1,3},{2,4},{3,5},{4,6},{5,7},{6,0},{7,1},{8,10},{9,11},{10,... | collective-permute-start | bytes 110600 | tf_op jit(solution)/shard_map/ppermute | solution.py:283
  60.8 16.8 %collective-permute-start = (bf16[16,1152]{1,0:T(8,128)(2,1)S(1)}, bf16[16,1152]{1,0:T(8,128)(2,1)S(1)}, u32[]{:S(2)}, u32[]{:S(2)}) collective-permute-start(bf16[16,1152]{1,0:T(8,128)(2,1)S(1)} %get-tuple-element.39), channel_id=1, source_target_pairs={{0,1},{1,2},{2,3},{3,4},{4,5},{5,6},{6,7},{7,0},{8,9},{9,10},{10,1... | collective-permute-start | bytes 110600 | tf_op jit(solution)/shard_map/ppermute | solution.py:283
  60.8 1.3 %copy-start = (bf16[256,2304]{1,0:T(8,128)(2,1)S(1)}, bf16[256,2304]{1,0:T(8,128)(2,1)}, u32[]{:S(2)}) copy-start(bf16[256,2304]{1,0:T(8,128)(2,1)} %get-tuple-element.17.hidden) | copy-start | bytes 3538948
  62.1 1.3 %copy-start.1 = (bf16[256,2304]{1,0:T(8,128)(2,1)S(1)}, bf16[256,2304]{1,0:T(8,128)(2,1)}, u32[]{:S(2)}) copy-start(bf16[256,2304]{1,0:T(8,128)(2,1)} %get-tuple-element.15.grad_gate_pre) | copy-start | bytes 3538948
  63.4 1.3 %copy-start.2 = (bf16[256,2304]{1,0:T(8,128)(2,1)S(1)}, bf16[256,2304]{1,0:T(8,128)(2,1)}, u32[]{:S(2)}) copy-start(bf16[256,2304]{1,0:T(8,128)(2,1)} %get-tuple-element.16.grad_up_pre) | copy-start | bytes 3538948
  64.6 1.1 %copy-start.3 = (bf16[256,1152]{1,0:T(8,128)(2,1)S(1)}, bf16[256,1152]{1,0:T(8,128)(2,1)}, u32[]{:S(2)}) copy-start(bf16[256,1152]{1,0:T(8,128)(2,1)} %get-tuple-element.14.features) | copy-start | bytes 1769476
  65.7 1.1 %copy-start.4 = (bf16[256,1152]{1,0:T(8,128)(2,1)S(1)}, bf16[256,1152]{1,0:T(8,128)(2,1)}, u32[]{:S(2)}) copy-start(bf16[256,1152]{1,0:T(8,128)(2,1)} %get-tuple-element.18.upstream) | copy-start | bytes 1769476

commit v2 on v1

--- a/solution.py
+++ b/solution.py
@@ -32,23 +32,29 @@
 
 
 def hidden_kernel(
-    loop, width, chunks,
+    loop, width, chunks, pieces,
     tokens, grad_out, gate_w, up_w, down_w,
-    features, upstream, hidden, grad_gate_pre, grad_up_pre, terms,
-    held, gate_v, up_v, down_v, own, sent, got, total,
+    features, upstream, hidden, grad_gate_pre, grad_up_pre, grad_tokens,
+    held, gate_v, up_v, down_v, own, sent, got, hidden_v, gate_pre_v, up_pre_v,
+    total, y_out, y_in, z_out, z_in, dp_out, final,
     load_sem, half_send, half_recv, ring_send, ring_recv, part_send, part_recv,
+    store_sem, y_send, y_recv, z_send, z_recv, dp_send, dp_recv,
 ):
     g, c, l = lax.axis_index("groups"), lax.axis_index("dp"), lax.axis_index("loop")
     depth = loop // width
     z, y = l // width, l % width
     rows, half = tokens.shape[0], gate_w.shape[0]
-    chunk = gate_v.shape[2]
+    units = gate_w.shape[1]
+    chunk, piece = units // chunks, half // pieces
     count = loop * 2 * rows
 
     def load(k, i):
-        cols = pl.ds(i * chunk, chunk)
-        source = down_w.at[cols] if k == 2 else (gate_w, up_w)[k].at[:, cols]
-        return pltpu.make_async_copy(source, (gate_v, up_v, down_v)[k].at[i], load_sem.at[k, i])
+        cols = pl.ds(pl.multiple_of(i * chunk, chunk), chunk)
+        if k == 2:
+            source, target = down_w.at[cols], down_v.at[cols]
+        else:
+            source, target = (gate_w, up_w)[k].at[:, cols], (gate_v, up_v)[k].at[:, cols]
+        return pltpu.make_async_copy(source, target, load_sem.at[k, i])
 
     barrier = pltpu.get_barrier_semaphore()
 
@@ -58,13 +64,12 @@
     greet((g, 1 - c, l))
     if width == 2:
         greet((g, c, z * width + 1 - y))
-    pl.when(z > 0)(lambda: greet((g, c, l - width)))
-    pl.when(z < depth - 1)(lambda: greet((g, c, l + width)))
-    inner = jnp.where(z > 0, 1, 0) + jnp.where(z < depth - 1, 1, 0)
+    for k in range(1, depth):
+        greet((g, c, lax.rem(z + k, depth) * width + y))
     for k in range(3):
         for i in range(chunks):
             load(k, i).start()
-    pl.semaphore_wait(barrier, (2 if width == 2 else 1) + inner)
+    pl.semaphore_wait(barrier, (2 if width == 2 else 1) + depth - 1)
 
     mine = pl.ds(pl.multiple_of(c * rows, rows), rows)
     kept = pl.ds(pl.multiple_of(c * half, 128), half)
@@ -139,10 +144,12 @@
         def step(i, carry):
             load(k, i).wait()
             x = held[min(1, k // 2)].reshape(count, half)
+            cols = pl.ds(pl.multiple_of(i * chunk, chunk), chunk)
             if k == 2:
-                term = contract_last(x, down_v[i])
+                term = contract_last(x, down_v[cols, :])
             else:
-                term = jnp.dot(x, (gate_v, up_v)[k][i], preferred_element_type=jnp.float32)
+                weight = (gate_v, up_v)[k][:, cols]
+                term = jnp.dot(x, weight, preferred_element_type=jnp.float32)
             own[k, i] = term
             sent[k, i] = term.astype(jnp.bfloat16)
             part(k, i).start()
@@ -155,29 +162,91 @@
     forward(1)
     across(1)
     forward(2)
-    for a, out in enumerate((features, upstream)):
-        out[...] = held[a].reshape(count, half)
-    total[...] = jnp.zeros_like(total)
 
     def back(i, carry):
         whole = []
         for k in range(3):
             part(k, i).wait_recv()
             whole.append(own[k, i] + got[k, i].astype(jnp.float32))
-        h, gg, gu = pointwise(*whole)
         cols = pl.ds(pl.multiple_of(i * chunk, chunk), chunk)
-        hidden[:, cols] = h
-        grad_gate_pre[:, cols] = gg
-        grad_up_pre[:, cols] = gu
-        total[...] += contract_last(gg, gate_v[i]) + contract_last(gu, up_v[i])
+        hidden_v[:, cols], gate_pre_v[:, cols], up_pre_v[:, cols] = pointwise(*whole)
         return carry
 
     lax.fori_loop(0, chunks, back, 0)
-    for k in range(loop):
-        to = lax.rem(l + k, loop) * 2
+    stores = [
+        pltpu.make_async_copy(source, target, store_sem.at[k])
+        for k, (source, target) in enumerate((
+            (held.at[0], features), (held.at[1], upstream),
+            (hidden_v, hidden), (gate_pre_v, grad_gate_pre), (up_pre_v, grad_up_pre),
+        ))
+    ]
+    for store in stores:
+        store.start()
+
+    def block_rows(level, side):
+        return pl.ds(pl.multiple_of((level * width + side) * 2 * rows, 2 * rows), 2 * rows)
+
+    def over_y(p):
+        return pltpu.make_async_remote_copy(
+            src_ref=y_out.at[p], dst_ref=y_in.at[p],
+            send_sem=y_send.at[p], recv_sem=y_recv.at[p],
+            device_id=(g, c, z * width + 1 - y), device_id_type=MESH,
+        )
+
+    def over_z(p, k):
+        return pltpu.make_async_remote_copy(
+            src_ref=z_out.at[p, k], dst_ref=z_in.at[p, k],
+            send_sem=z_send.at[p, k], recv_sem=z_recv.at[p, k],
+            device_id=(g, c, lax.rem(z + k, depth) * width + y), device_id_type=MESH,
+        )
+
+    def over_dp(p):
+        cols = pl.ds(pl.multiple_of(c * half + p * piece, 128), piece)
+        return pltpu.make_async_remote_copy(
+            src_ref=dp_out.at[p], dst_ref=final.at[:, cols],
+            send_sem=dp_send.at[p], recv_sem=dp_recv.at[p],
+            device_id=(g, 1 - c, l), device_id_type=MESH,
+        )
+
+    for p in range(pieces):
+        part_rows = pl.ds(p * piece, piece)
+        total[p] = contract_last(gate_pre_v[...], gate_v[part_rows, :])
+        total[p] += contract_last(up_pre_v[...], up_v[part_rows, :])
+        if width == 2:
+            for k in range(depth):
+                y_out[p, k] = total[p, block_rows(k, 1 - y), :].astype(jnp.bfloat16)
+            over_y(p).start()
+    for p in range(pieces):
+        if width == 2:
+            over_y(p).wait_recv()
+        for k in list(range(1, depth)) + [0]:
+            to = lax.rem(z + k, depth)
+            term = total[p, block_rows(to, y), :]
+            if width == 2:
+                term += y_in[p, to].astype(jnp.float32)
+            if k:
+                z_out[p, k] = term.astype(jnp.bfloat16)
+                over_z(p, k).start()
+            else:
+                total[p, block_rows(z, y), :] = term
+    for p in range(pieces):
+        for k in range(1, depth):
+            over_z(p, k).wait_recv()
         for e in range(2):
-            at = to + (c if e == 0 else 1 - c)
-            terms[e, k] = total[pl.ds(pl.multiple_of(at * rows, rows), rows), :].astype(jnp.bfloat16)
+            side = c if e else 1 - c
+            start = pl.multiple_of((l * 2 + side) * rows, rows)
+            term = total[p, pl.ds(start, rows), :]
+            for k in range(1, depth):
+                term += z_in[p, k, pl.ds(pl.multiple_of(side * rows, rows), rows), :].astype(jnp.float32)
+            if e:
+                cols = pl.ds(pl.multiple_of(c * half + p * piece, 128), piece)
+                final[:, cols] = term.astype(jnp.bfloat16)
+            else:
+                dp_out[p] = term.astype(jnp.bfloat16)
+                over_dp(p).start()
+    for p in range(pieces):
+        over_dp(p).wait_recv()
+    grad_tokens[...] = final[...]
 
     def drain(i, carry):
         for k in range(3):
@@ -189,35 +258,55 @@
         swap(a).wait_send()
         for d in range(depth):
             sends(a, d, "wait_send")
+    for p in range(pieces):
+        if width == 2:
+            over_y(p).wait_send()
+        for k in range(1, depth):
+            over_z(p, k).wait_send()
+        over_dp(p).wait_send()
+    for store in stores:
+        store.wait()
 
 
 def find_hidden(loop, width, tokens, grad_out, gate_weight, up_weight, down_weight):
     rows = tokens.shape[0]
     half, units = gate_weight.shape
-    count = loop * 2 * rows
+    count, depth = loop * 2 * rows, loop // width
     chunk = next((n for n in (384, 256, 128) if units % n == 0), units)
-    chunks = units // chunk
+    piece = next((n for n in (384, 256, 128) if half % n == 0), half)
+    chunks, pieces = units // chunk, half // piece
     bf16, f32 = jnp.bfloat16, jnp.float32
     vmem, far = pl.BlockSpec(memory_space=pltpu.VMEM), pl.BlockSpec(memory_space=pl.ANY)
     dma = pltpu.SemaphoreType.DMA
     return pl.pallas_call(
-        functools.partial(hidden_kernel, loop, width, chunks),
-        out_shape=[jax.ShapeDtypeStruct((count, half), bf16)] * 2
+        functools.partial(hidden_kernel, loop, width, chunks, pieces),
+        out_shape=[jax.ShapeDtypeStruct((loop, 2 * rows, half), bf16)] * 2
         + [jax.ShapeDtypeStruct((count, units), bf16)] * 3
-        + [jax.ShapeDtypeStruct((2, loop, rows, half), bf16)],
+        + [jax.ShapeDtypeStruct((rows, 2 * half), bf16)],
         in_specs=[vmem, vmem, far, far, far],
-        out_specs=[vmem] * 6,
+        out_specs=[far] * 5 + [vmem],
         scratch_shapes=[
             pltpu.VMEM((2, loop, 2 * rows, half), bf16),
-            pltpu.VMEM((chunks, half, chunk), bf16),
-            pltpu.VMEM((chunks, half, chunk), bf16),
-            pltpu.VMEM((chunks, chunk, half), bf16),
+            pltpu.VMEM((half, units), bf16),
+            pltpu.VMEM((half, units), bf16),
+            pltpu.VMEM((units, half), bf16),
             pltpu.VMEM((3, chunks, count, chunk), f32),
             pltpu.VMEM((3, chunks, count, chunk), bf16),
             pltpu.VMEM((3, chunks, count, chunk), bf16),
-            pltpu.VMEM((count, half), f32),
+            pltpu.VMEM((count, units), bf16),
+            pltpu.VMEM((count, units), bf16),
+            pltpu.VMEM((count, units), bf16),
+            pltpu.VMEM((pieces, count, piece), f32),
+            pltpu.VMEM((pieces, depth, 2 * rows, piece), bf16),
+            pltpu.VMEM((pieces, depth, 2 * rows, piece), bf16),
+            pltpu.VMEM((pieces, depth, 2 * rows, piece), bf16),
+            pltpu.VMEM((pieces, depth, 2 * rows, piece), bf16),
+            pltpu.VMEM((pieces, rows, piece), bf16),
+            pltpu.VMEM((rows, 2 * half), bf16),
             dma((3, chunks)), dma((2,)), dma((2,)),
             dma((2, loop, 3)), dma((2, loop)), dma((3, chunks)), dma((3, chunks)),
+            dma((5,)), dma((pieces,)), dma((pieces,)),
+            dma((pieces, depth)), dma((pieces, depth)), dma((pieces,)), dma((pieces,)),
         ],
         compiler_params=pltpu.CompilerParams(
             collective_id=0, has_side_effects=True, vmem_limit_bytes=58 * MIB
@@ -268,36 +357,15 @@
     )(features, grad_gate_pre, grad_up_pre, hidden, upstream)
 
 
-def sum_terms(loop, terms):
-    halves = []
-    for e in range(2):
-        total = None
-        for k in range(loop):
-            term = terms[e, k]
-            if e or k:
-                pairs = [
-                    (c * loop + l, (c ^ e) * loop + (l + k) % loop)
-                    for c in range(2)
-                    for l in range(loop)
-                ]
-                term = lax.ppermute(term, ("dp", "loop"), pairs)
-            term = term.astype(jnp.float32)
-            total = term if total is None else total + term
-        halves.append(total)
-    kept, other = halves
-    first = lax.axis_index("dp") == 0
-    low, high = jnp.where(first, kept, other), jnp.where(first, other, kept)
-    return jnp.concatenate([low, high], axis=1).astype(jnp.bfloat16)
-
-
 def on_device(loop, width, tokens, grad_out, gate_weight, up_weight, down_weight):
-    features, upstream, hidden, grad_gate_pre, grad_up_pre, terms = find_hidden(
+    features, upstream, hidden, grad_gate_pre, grad_up_pre, grad_tokens = find_hidden(
         loop, width, tokens, grad_out, gate_weight, up_weight, down_weight
     )
+    features, upstream = (x.reshape(-1, x.shape[2]) for x in (features, upstream))
     grad_gate, grad_up, grad_down = weight_gradients(
         features, upstream, hidden, grad_gate_pre, grad_up_pre
     )
-    return (sum_terms(loop, terms), grad_gate, grad_up, grad_down)
+    return (grad_tokens, grad_gate, grad_up, grad_down)
 
 
 def columns(mesh):

time: 79.6 us -> 68.2 us (0.86)
  starting transfers between devices: 18.5 us -> 0 us
  Pallas kernels: 51.4 us -> 60.6 us
  other arithmetic: 1.51 us -> 0 us
    ppermute x15 -> x0, starting transfers between devices: 18.5 us -> none  [sum_terms(): term = lax.ppermute(term, ('dp', 'loop'), pairs)]
    pallas_call x1, Pallas kernels: 40.6 us -> 49.8 us  [find_hidden(): pl.pallas_call(functools.partial(hidden_kernel, loop, width, chunks, piec...]
    squeeze x1 -> x0, local copies, waits for them, and re-layouts: 1.07 us -> none  [sum_terms(): term = terms[e, k]]
    another operation x2 -> x0, other arithmetic: 0.87 us -> none
    unnamed x10 -> x13, local copies, waits for them, and re-layouts: 5.94 us -> 6.57 us
  transfers between devices with their start and end apart: 15 -> 0, of which waited for: 0 -> 0; matrix products, arithmetic and copies ran while one was open for 0% -> 0% of each run, Pallas kernels for 14% -> 0%
where the time goes in v2:
time: 68.2 us; the launch traced here: 67.8 us
  Pallas kernels  60.6 us (89%)
  local copies, waits for them, and re-layouts  6.57 us (10%)
    pallas_call x1, Pallas kernels, find_hidden(): pl.pallas_call(functools.partial(hidden_kernel, loop, width, chunks, piec...  49.8 us
    pallas_call x1, Pallas kernels, weight_gradients(): pl.pallas_call(gradient_kernel, grid=(steps,), out_shape=[jax.ShapeDtypeS...  10.8 us
    unnamed x13, local copies, waits for them, and re-layouts  6.57 us

profile of v2, /device:TPU:0, one launch (start us, length us, event | category | flops | bytes accessed | tf_op | source)
XLA Modules:
  0.0 67.8 jit_solution(14979046897203158238)
XLA Ops:
  0.6 49.8 %find_hidden.1 = (bf16[8,32,1152]{2,1,0:T(8,128)(2,1)}, bf16[8,32,1152]{2,1,0:T(8,128)(2,1)}, bf16[256,2304]{1,0:T(8,128)(2,1)}, bf16[256,2304]{1,0:T(8,128)(2,1...) custom-call(bf16[16,2304]{1,0:T(8,128)(2,1)} %tokens.1, bf16[16,2304]{1,0:T(8,128)(2,1)} %grad_out.1, ...), custom_call_target="tpu_custom_call" | custom-call | flops 6794772480 | bytes 24772608 | tf_op jit(solution)/shard_map/find_hidden/pallas_call | solution.py:281
  50.4 0.0 copy-start
  50.4 1.1 %copy-done = bf16[8,32,1152]{2,1,0:T(8,128)(2,1)S(1)} copy-done((bf16[8,32,1152]{2,1,0:T(8,128)(2,1)S(1)}, bf16[8,32,1152]{2,1,0:T(8,128)(2,1)}, u32[]{:S(2)}) %copy-start) | copy-done | bytes 589848
  51.5 0.0 copy-start.1
  51.5 1.1 %copy-done.1 = bf16[8,32,1152]{2,1,0:T(8,128)(2,1)S(1)} copy-done((bf16[8,32,1152]{2,1,0:T(8,128)(2,1)S(1)}, bf16[8,32,1152]{2,1,0:T(8,128)(2,1)}, u32[]{:S(2)}) %copy-start.1) | copy-done | bytes 589848
  52.6 0.0 copy-start.2
  52.6 1.3 %copy-done.2 = bf16[256,2304]{1,0:T(8,128)(2,1)S(1)} copy-done((bf16[256,2304]{1,0:T(8,128)(2,1)S(1)}, bf16[256,2304]{1,0:T(8,128)(2,1)}, u32[]{:S(2)}) %copy-start.2) | copy-done | bytes 1179672
  53.8 0.0 copy-start.3
  53.8 1.3 %copy-done.3 = bf16[256,2304]{1,0:T(8,128)(2,1)S(1)} copy-done((bf16[256,2304]{1,0:T(8,128)(2,1)S(1)}, bf16[256,2304]{1,0:T(8,128)(2,1)}, u32[]{:S(2)}) %copy-start.3) | copy-done | bytes 1179672
  55.1 0.0 copy-start.4
  55.1 1.3 %copy-done.4 = bf16[256,2304]{1,0:T(8,128)(2,1)S(1)} copy-done((bf16[256,2304]{1,0:T(8,128)(2,1)S(1)}, bf16[256,2304]{1,0:T(8,128)(2,1)}, u32[]{:S(2)}) %copy-start.4) | copy-done | bytes 1179672
  56.4 0.0 copy-start.5
  56.4 10.8 %weight_gradients.1 = (f32[1152,2304]{1,0:T(8,128)}, f32[1152,2304]{1,0:T(8,128)}, f32[2304,1152]{1,0:T(8,128)}) custom-call(bf16[256,1152]{1,0:T(8,128)(2,1)S(1)} %bitcast.2, bf16[256,2304]{1,0:T(8,128)(2,1)S(1)} %copy-done.3, bf16[256,2304]{1,0:T(8,128)(2,1)S(1)} %copy-done.4, bf16[256,2304]{1,0:T(8,128)(2,1)S(1)} %copy-done.2, bf16[256,1152]{1,0:T(8,128)(2,1)S(1)} %bitcast.3), custom_call_target="tpu_custom_call" | custom-call | flops 4076863488 | bytes 36569088 | tf_op jit(solution)/shard_map/weight_gradients/pallas_call | solution.py:343
  67.2 0.0 copy-done.5
  67.2 0.6 copy.10
Async XLA Ops:
  50.4 1.1 %copy-start = (bf16[8,32,1152]{2,1,0:T(8,128)(2,1)S(1)}, bf16[8,32,1152]{2,1,0:T(8,128)(2,1)}, u32[]{:S(2)}) copy-start(bf16[8,32,1152]{2,1,0:T(8,128)(2,1)} %get-tuple-element.14) | copy-start | bytes 1769476
  51.5 1.1 %copy-start.1 = (bf16[8,32,1152]{2,1,0:T(8,128)(2,1)S(1)}, bf16[8,32,1152]{2,1,0:T(8,128)(2,1)}, u32[]{:S(2)}) copy-start(bf16[8,32,1152]{2,1,0:T(8,128)(2,1)} %get-tuple-element.18) | copy-start | bytes 1769476
  52.6 1.3 %copy-start.2 = (bf16[256,2304]{1,0:T(8,128)(2,1)S(1)}, bf16[256,2304]{1,0:T(8,128)(2,1)}, u32[]{:S(2)}) copy-start(bf16[256,2304]{1,0:T(8,128)(2,1)} %get-tuple-element.17.hidden) | copy-start | bytes 3538948
  53.8 1.3 %copy-start.3 = (bf16[256,2304]{1,0:T(8,128)(2,1)S(1)}, bf16[256,2304]{1,0:T(8,128)(2,1)}, u32[]{:S(2)}) copy-start(bf16[256,2304]{1,0:T(8,128)(2,1)} %get-tuple-element.15.grad_gate_pre) | copy-start | bytes 3538948
  55.1 1.3 %copy-start.4 = (bf16[256,2304]{1,0:T(8,128)(2,1)S(1)}, bf16[256,2304]{1,0:T(8,128)(2,1)}, u32[]{:S(2)}) copy-start(bf16[256,2304]{1,0:T(8,128)(2,1)} %get-tuple-element.16.grad_up_pre) | copy-start | bytes 3538948
  56.4 10.8 %copy-start.5 = (bf16[16,2304]{1,0:T(8,128)(2,1)S(1)}, bf16[16,2304]{1,0:T(8,128)(2,1)}, u32[]{:S(2)}) copy-start(bf16[16,2304]{1,0:T(8,128)(2,1)} %get-tuple-element.26) | copy-start | bytes 221188

commit v3 on v2

--- a/solution.py
+++ b/solution.py
@@ -66,9 +66,6 @@
         greet((g, c, z * width + 1 - y))
     for k in range(1, depth):
         greet((g, c, lax.rem(z + k, depth) * width + y))
-    for k in range(3):
-        for i in range(chunks):
-            load(k, i).start()
     pl.semaphore_wait(barrier, (2 if width == 2 else 1) + depth - 1)
 
     mine = pl.ds(pl.multiple_of(c * rows, rows), rows)
@@ -128,9 +125,16 @@
                 move(a, k * width + 1 - y, 2).wait_recv()
 
     sends(0, 0, "start")
-    for d in range(1, depth):
+    sends(1, 0, "start")
+    sends(0, 1, "start")
+    sends(1, 1, "start")
+    for k in range(3):
+        for i in range(chunks):
+            load(k, i).start()
+    for d in range(2, depth):
         sends(0, d, "start")
-        sends(1, d - 1, "start")
+        if d < depth - 1:
+            sends(1, d, "start")
     across(0)
 
     def part(k, i):
@@ -272,7 +276,7 @@
     rows = tokens.shape[0]
     half, units = gate_weight.shape
     count, depth = loop * 2 * rows, loop // width
-    chunk = next((n for n in (384, 256, 128) if units % n == 0), units)
+    chunk = next((n for n in (768, 384, 256, 128) if units % n == 0), units)
     piece = next((n for n in (384, 256, 128) if half % n == 0), half)
     chunks, pieces = units // chunk, half // piece
     bf16, f32 = jnp.bfloat16, jnp.float32
@@ -347,7 +351,7 @@
         + [jax.ShapeDtypeStruct((units, half), jnp.float32)],
         in_specs=[slab(tall), whole(units), whole(units), slab(wide), whole(half)],
         out_specs=[rows(tall, units), rows(tall, units), rows(wide, half)],
-        compiler_params=pltpu.CompilerParams(vmem_limit_bytes=40 * MIB),
+        compiler_params=pltpu.CompilerParams(vmem_limit_bytes=58 * MIB),
         cost_estimate=pl.CostEstimate(
             flops=6 * count * half * units,
             bytes_accessed=12 * half * units + 2 * count * (3 * units + 2 * half),

time: 68.2 us -> 62 us (0.909)
  local copies, waits for them, and re-layouts: 6.57 us -> 0.64 us
    unnamed x13 -> x3, local copies, waits for them, and re-layouts: 6.57 us -> 0.64 us
    pallas_call x1, Pallas kernels: 49.8 us -> 47.5 us  [find_hidden(): pl.pallas_call(functools.partial(hidden_kernel, loop, width, chunks, piec...]
    pallas_call x1, Pallas kernels: 10.8 us -> 12.9 us  [weight_gradients(): pl.pallas_call(gradient_kernel, grid=(steps,), out_shape=[jax.ShapeDtypeS...]
where the time goes in v3:
time: 62 us; the launch traced here: 61.6 us
  Pallas kernels  60.3 us (97%)
  between operations  0.65 us (1%)
  local copies, waits for them, and re-layouts  0.64 us (1%)
    pallas_call x1, Pallas kernels, find_hidden(): pl.pallas_call(functools.partial(hidden_kernel, loop, width, chunks, piec...  47.5 us
    pallas_call x1, Pallas kernels, weight_gradients(): pl.pallas_call(gradient_kernel, grid=(steps,), out_shape=[jax.ShapeDtypeS...  12.9 us

profile of v3, /device:TPU:0, one launch (start us, length us, event | category | flops | bytes accessed | tf_op | source)
XLA Modules:
  0.0 61.6 jit_solution(10116276547115768240)
XLA Ops:
  0.6 47.5 %find_hidden.1 = (bf16[8,32,1152]{2,1,0:T(8,128)(2,1)}, bf16[8,32,1152]{2,1,0:T(8,128)(2,1)}, bf16[256,2304]{1,0:T(8,128)(2,1)}, bf16[256,2304]{1,0:T(8,128)(2,1...) custom-call(bf16[16,2304]{1,0:T(8,128)(2,1)} %tokens.1, bf16[16,2304]{1,0:T(8,128)(2,1)} %grad_out.1, ...), custom_call_target="tpu_custom_call" | custom-call | flops 6794772480 | bytes 24772608 | tf_op jit(solution)/shard_map/find_hidden/pallas_call | solution.py:285
  48.1 0.0 copy-start
  48.1 12.9 %weight_gradients.1 = (f32[1152,2304]{1,0:T(8,128)}, f32[1152,2304]{1,0:T(8,128)}, f32[2304,1152]{1,0:T(8,128)}) custom-call(bf16[256,1152]{1,0:T(8,128)(2,1)} %bitcast.2, bf16[256,2304]{1,0:T(8,128)(2,1)} %get-tuple-element.15.grad_gate_pre, bf16[256,2304]{1,0:T(8,128)(2,1)} %get-tuple-element.16.grad_up_pre, bf16[256,2304]{1,0:T(8,128)(2,1)} %get-tuple-element.17.hidden, ...), custom_call_target="tpu_custom_call" | custom-call | flops 4076863488 | bytes 36569088 | tf_op jit(solution)/shard_map/weight_gradients/pallas_call | solution.py:347
  61.0 0.0 copy-done
  61.0 0.6 %copy.10 = bf16[16,2304]{1,0:T(8,128)(2,1)} copy(bf16[16,2304]{1,0:T(8,128)(2,1)S(1)} %copy-done) | data formatting | bytes 147456
Async XLA Ops:
  48.1 12.9 %copy-start = (bf16[16,2304]{1,0:T(8,128)(2,1)S(1)}, bf16[16,2304]{1,0:T(8,128)(2,1)}, u32[]{:S(2)}) copy-start(bf16[16,2304]{1,0:T(8,128)(2,1)} %get-tuple-element.26) | copy-start | bytes 221188
